TPU v7x, 32 devices: a whole 2x2x4 slice. The times are simulated.
32 devices in a mesh: seq: 2 (over x), row: 4 (over y, core), col: 4 (over z).
Axes of the slice: x: 2, y: 2, z: 4, core: 2. Of those that a mesh axis runs over, the one named last changes fastest.
Arguments:
- inputs: bfloat16 [4, 16, 64, 4096], P('row', 'seq', None, 'col'), may hold values from -8 to 8
- query_proj: bfloat16 [4, 16, 64, 4096], P('row', 'seq', None, 'col'), may hold values from -5 to 5
- key_proj: bfloat16 [4, 16, 64, 4096], P('row', 'seq', None, 'col'), may hold values from -5 to 5
- value_proj: bfloat16 [4, 16, 64, 4096], P('row', 'seq', None, 'col'), may hold values from -6 to 6
- depth_weight: bfloat16 [7, 7, 4096], P(None, None, 'col'), may hold values from -1.25 to 1.25
- depth_bias: bfloat16 [4096], P('col'), may hold values from -3 to 3
- norm_gain: bfloat16 [4096], replicated, may hold values from 0.099609375 to 1.8984375
- norm_bias: bfloat16 [4096], replicated, may hold values from -3 to 3
- expand_weight: bfloat16 [4096, 16384], P(('seq', 'row'), 'col'), may hold values from -0.09375 to 0.09375
- expand_bias: bfloat16 [16384], P('col'), may hold values from -3 to 3
Outputs:
- residual_out: bfloat16 [4, 16, 64, 4096], P('row', 'seq', None, 'col')
- hidden: bfloat16 [4, 16, 64, 16384], P('row', 'seq', None, 'col')
All inputs are finite; a program needn't handle non-finite values.
Results may differ from a plain program's by a relative error of at most 0.0075.
Values may be sent and summed in bfloat16 or wider, within the bound.
A program may use at most 128 MiB of HBM per device.

v0:
```python
import math

import jax
import jax.numpy as jnp
from jax import lax
from jax.sharding import PartitionSpec as P

HEAD_DIM = 128
KERNEL = 7


def padded_2(array, sides, width):
    for axis, dim in sides:
        peers, length = (lax.axis_size(axis), array.shape[dim])
        up = [(i, (i + 1) % peers) for i in range(peers - 1)]
        down = [(j, i) for i, j in up]
        last = lax.slice_in_dim(array, length - width, length, axis=dim)
        leading = lax.slice_in_dim(array, 0, width, axis=dim)
        before = lax.ppermute(last, axis, up)
        after = lax.ppermute(leading, axis, down)
        array = jnp.concatenate([before, array, after], axis=dim)
    return array


def on_device(
    inputs,
    query_proj,
    key_proj,
    value_proj,
    depth_weight,
    depth_bias,
    norm_gain,
    norm_bias,
    expand_weight,
    expand_bias,
):
    samples, rows_here, col_count, channels = inputs.shape
    heads_here = channels // HEAD_DIM
    positions = rows_here * col_count
    score_scale = 1.0 / math.sqrt(HEAD_DIM)
    queries = query_proj.reshape(samples, positions, heads_here, HEAD_DIM)
    start_max = jnp.full((samples, heads_here, positions), -1e30, jnp.float32)
    keys_in = lax.all_gather(key_proj, "seq", axis=1, tiled=True)
    values_in = lax.all_gather(value_proj, "seq", axis=1, tiled=True)
    count = keys_in.shape[1] * keys_in.shape[2]
    keys_in = keys_in.reshape(samples, count, heads_here, HEAD_DIM)
    values_in = values_in.reshape(samples, count, heads_here, HEAD_DIM)
    scores = (
        jnp.einsum("bqhd,bkhd->bhqk", queries, keys_in, preferred_element_type=jnp.float32)
        * score_scale
    )
    new_max = jnp.maximum(start_max, jnp.max(scores, axis=-1))
    weights = jnp.exp(scores - new_max[..., None])
    new_total = jnp.sum(weights, axis=-1)
    update = jnp.einsum(
        "bhqk,bkhd->bhqd",
        weights.astype(jnp.bfloat16),
        values_in,
        preferred_element_type=jnp.float32,
    )
    attended = update / new_total[..., None]
    attended = jnp.transpose(attended, (0, 2, 1, 3)).reshape(
        samples, rows_here, col_count, channels
    )
    residual_out = (inputs.astype(jnp.float32) + attended).astype(jnp.bfloat16)
    margin = KERNEL // 2
    padded = padded_2(residual_out, (("seq", 1),), margin)
    padded = jnp.pad(padded, ((0, 0), (0, 0), (margin, margin), (0, 0))).astype(jnp.float32)
    kernel_taps = depth_weight.astype(jnp.float32)
    convolved = jnp.zeros((samples, rows_here, col_count, channels), jnp.float32)
    for row_tap in range(KERNEL):
        for col_tap in range(KERNEL):
            convolved = (
                convolved
                + padded[:, row_tap : row_tap + rows_here, col_tap : col_tap + col_count, :]
                * kernel_taps[row_tap, col_tap]
            )
    convolved = (convolved + depth_bias.astype(jnp.float32)).astype(jnp.bfloat16)
    flat_rows = convolved.reshape(samples * positions, channels)
    gathered = lax.all_gather(flat_rows, "col", axis=1, tiled=True)
    widened = gathered.astype(jnp.float32)
    center = jnp.mean(widened, axis=1, keepdims=True)
    spread = jnp.mean((widened - center) * (widened - center), axis=1, keepdims=True)
    normed = (
        (widened - center) * lax.rsqrt(spread + 1e-06) * norm_gain.astype(jnp.float32)
        + norm_bias.astype(jnp.float32)
    ).astype(jnp.bfloat16)
    project = jnp.dot(
        normed,
        lax.all_gather(expand_weight, ("seq", "row"), axis=0, tiled=True),
        preferred_element_type=jnp.float32,
    )
    hidden = jax.nn.gelu(project + expand_bias.astype(jnp.float32), approximate=False).astype(
        jnp.bfloat16
    )
    return (residual_out, hidden.reshape(samples, rows_here, col_count, expand_weight.shape[1]))


def solution(mesh):
    return jax.shard_map(
        on_device,
        mesh=mesh,
        in_specs=(
            P("row", "seq", None, "col"),
            P("row", "seq", None, "col"),
            P("row", "seq", None, "col"),
            P("row", "seq", None, "col"),
            P(None, None, "col"),
            P("col"),
            P(),
            P(),
            P(("seq", "row"), "col"),
            P("col"),
        ),
        out_specs=(P("row", "seq", None, "col"), P("row", "seq", None, "col")),
        check_vma=False,
    )
```

profile of v0, /device:TPU:1, one launch (start us, length us, event | category | flops | bytes accessed | tf_op | source)
XLA Modules:
  0.0 462.3 jit_solution(17272596867813315271)
XLA Ops:
  7.2 0.0 copy-start.3
  7.2 0.0 all-gather.5.cloned.1.call-start
  7.2 0.0 copy-start.9
  7.2 0.0 copy-start.5
  7.2 0.7 all-gather.5.cloned.1.call-update
  7.9 0.0 all-gather.7.cloned.1.call-start
  8.0 0.7 all-gather.7.cloned.1.call-update
  8.7 0.0 all-gather.9.cloned.1.call-start
  8.7 0.0 copy-done.3
  8.7 0.3 copy.44
  9.0 0.0 copy-done.9
  9.0 0.0 copy-done.5
  9.0 0.1 fusion.95
  9.1 35.7 %all-gather.5.cloned.1.call-done = bf16[1,16,64,1024]{3,2,0,1:T(8,128)(2,1)} async-done(((bf16[1,8,64,1024]{3,2,0,1:T(8,128)(2,1)}), bf16[1,16,64,1024]{3,2,0,1:T(8,128)(2,1)}) %all-gather.5.cloned.1.call-update) | async-done | bytes 2097168 | tf_op jit(solution)/shard_map/all_gather | solution.py:43
  44.8 2.2 copy.45
  47.0 7.3 %multiply_reduce_fusion = (f32[8,512]{1,0:T(8,128)S(1)}, f32[8,512,1024]{2,1,0:T(8,128)}) fusion(bf16[1024,8,128]{2,1,0:T(8,128)(2,1)S(1)} %bitcast.73, bf16[512,8,128]{2,1,0:T(8,128)(2,1)S(1)} %bitcast.75), kind=kOutput, calls=%fused_computation.1 | convolution fusion | flops 1082126336 | bytes 19939328 | tf_op jit(solution)/shard_map/bqhd,bkhd->bhqk/dot_general | solution.py:49
  54.3 25.2 %all-gather.7.cloned.1.call-done = bf16[1,16,64,1024]{3,2,0,1:T(8,128)(2,1)} async-done(((bf16[1,8,64,1024]{3,2,0,1:T(8,128)(2,1)}), bf16[1,16,64,1024]{3,2,0,1:T(8,128)(2,1)}) %all-gather.7.cloned.1.call-update) | async-done | bytes 2097168 | tf_op jit(solution)/shard_map/all_gather | solution.py:44
  79.5 2.2 copy.46
  81.7 0.0 copy-start
  81.7 7.8 %fusion = f32[8,512]{1,0:T(8,128)S(1)} fusion(f32[8,512,1024]{2,1,0:T(8,128)} %get-tuple-element.60, f32[8,512]{1,0:T(8,128)S(1)} %broadcast_maximum_fusion), kind=kLoop, calls=%fused_computation.2 | loop fusion | flops 12578816 | bytes 16809984 | tf_op jit(solution)/shard_map/reduce_sum | solution.py:54
  89.6 2.8 copy-done
  92.3 4.4 divide_bitcast_fusion
  96.8 0.0 copy-start.4
  96.8 1.2 copy.42
  98.0 0.0 copy-done.4
  98.0 0.7 fusion.81
  98.7 0.0 copy-start.2
  98.7 0.1 fusion.94
  98.8 2.1 collective-permute-start
  100.9 1.5 collective-permute-start.1
  102.5 0.1 fusion.96
  102.5 6.3 %collective-permute-done = bf16[1,3,64,1024]{3,2,1,0:T(8,128)(2,1)S(1)} collective-permute-done((bf16[1,3,64,1024]{3,2,1,0:T(8,128)(2,1)S(1)}, bf16[1,3,64,1024]{3,2,1,0:T(8,128)(2,1)S(1)}, u32[]{:S(2)}, u32[]{:S(2)}) %collective-permute-start) | collective-permute-done | bytes 393248 | tf_op jit(solution)/shard_map/ppermute | solution.py:19
  108.9 3.8 collective-permute-done.1
  112.7 2.6 fusion.87
  115.3 0.0 copy-done.2
  115.3 53.4 %fusion.33 = bf16[1,8,64,1024]{3,2,1,0:T(8,128)(2,1)} fusion(f32[1,14,70,1024]{3,2,1,0:T(8,128)} %fusion.87, f32[1024]{0:T(1024)S(1)} %convert_element_type.47, f32[1024]{0:T(1024)S(1)} %bitcast.112, f32[1024]{0:T(1024)S(1)} %bitcast.111, f32[1024]{0:T(1024)S(1)} %bitcast.110, f32[1024]{0:T(1024)S(1)} %bitcast.109, f32[1024]{0:T(1024)S(1)} %bitcast.108, ...), kind=kLoop, calls=%fused_computation.47 | loop fusion | flops 51904512 | bytes 104013824 | tf_op jit(solution)/shard_map/convert_element_type | solution.py:78
  168.7 0.0 all-gather.9.cloned.1.call-update
  168.8 0.0 copy-start.6
  168.8 0.0 copy-start.7
  168.8 0.0 copy-start.8
  168.8 0.0 all-gather.11.cloned.1.call-start
  168.8 0.5 all-gather.11.cloned.1.call-update
  169.4 0.1 copy-done.6
  169.5 0.0 copy-done.7
  169.5 0.0 copy-done.8
  169.5 81.3 %all-gather.9.cloned.1.call-done = bf16[512,4096]{1,0:T(8,128)(2,1)} async-done(((bf16[512,1024]{1,0:T(8,128)(2,1)}), bf16[512,4096]{1,0:T(8,128)(2,1)}) %all-gather.9.cloned.1.call-update) | async-done | bytes 4194320 | tf_op jit(solution)/shard_map/all_gather | solution.py:80
  250.8 0.0 copy-start.1
  250.8 3.0 convert_reduce_fusion
  253.7 0.5 copy-done.1
  254.2 1.2 fusion.4
  255.5 156.8 %all-gather.11.cloned.1.call-done = bf16[4096,4096]{1,0:T(8,128)(2,1)} async-done(((bf16[512,4096]{1,0:T(8,128)(2,1)}), bf16[4096,4096]{1,0:T(8,128)(2,1)}) %all-gather.11.cloned.1.call-update) | async-done | bytes 33554448 | tf_op jit(solution)/shard_map/all_gather | solution.py:90
  412.3 43.5 %fusion.10 = bf16[512,4096]{1,0:T(8,128)(2,1)} fusion(bf16[4096,4096]{1,0:T(8,128)(2,1)} %all-gather.11.cloned.1.call-done, bf16[512,4096]{1,0:T(8,128)(2,1)} %all-gather.9.cloned.1.call-done, f32[4096]{0:T(1024)S(1)} %convert_element_type.53, f32[4096]{0:T(1024)S(1)} %convert_element_type.51, f32[4096]{0:T(1024)S(1)} %convert_element_type.50, ...), kind=kOutput, calls=%fused_computation.15 | convolution fusion | flops 17330864128 | bytes 41996288 | tf_op jit(solution)/shard_map/dot_general | solution.py:88
  (8 shorter events, 0.1 us)
Async XLA Ops:
  7.2 1.5 copy-start.3
  7.2 37.6 %all-gather.5.cloned.1.call-start = ((), (), s32[]{:S(2)}) async-start(), calls=%async_computation | async-start | bytes 3145728 | tf_op jit(solution)/shard_map/all_gather | solution.py:43
  7.2 1.8 copy-start.9
  7.2 1.8 copy-start.5
  7.9 71.6 %all-gather.7.cloned.1.call-start = ((), (), s32[]{:S(2)}) async-start(), calls=%async_computation.1 | async-start | bytes 3145728 | tf_op jit(solution)/shard_map/all_gather | solution.py:44
  8.7 242.1 %all-gather.9.cloned.1.call-start = ((), (), s32[]{:S(2)}) async-start(), calls=%async_computation.2 | async-start | bytes 5242880 | tf_op jit(solution)/shard_map/all_gather | solution.py:80
  81.7 10.6 %copy-start = (f32[8,512,1024]{2,1,0:T(8,128)S(1)}, f32[8,512,1024]{2,1,0:T(8,128)}, u32[]{:S(2)}) copy-start(f32[8,512,1024]{2,1,0:T(8,128)} %get-tuple-element.60) | copy-start | bytes 50331652
  96.8 1.2 copy-start.4
  98.7 16.6 %copy-start.2 = (bf16[1,8,64,1024]{3,2,1,0:T(8,128)(2,1)}, bf16[1,8,64,1024]{3,2,1,0:T(8,128)(2,1)S(1)}, u32[]{:S(2)}) copy-start(bf16[1,8,64,1024]{3,2,1,0:T(8,128)(2,1)S(1)} %fusion.81) | copy-start | bytes 3145732
  98.8 10.1 %collective-permute-start = (bf16[1,3,64,1024]{3,2,1,0:T(8,128)(2,1)S(1)}, bf16[1,3,64,1024]{3,2,1,0:T(8,128)(2,1)S(1)}, u32[]{:S(2)}, u32[]{:S(2)}) collective-permute-start(bf16[1,3,64,1024]{3,2,1,0:T(8,128)(2,1)S(1)} %get-tuple-element.8), channel_id=1, source_target_pairs={{0,16},{1,17},{2,18},{3,19},{4,20},{5,21},{6,22},{7,23},{8,24},{9,... | collective-permute-start | bytes 1179656 | tf_op jit(solution)/shard_map/ppermute | solution.py:19
  100.9 11.7 %collective-permute-start.1 = (bf16[1,3,64,1024]{3,2,1,0:T(8,128)(2,1)S(1)}, bf16[1,3,64,1024]{3,2,1,0:T(8,128)(2,1)S(1)}, u32[]{:S(2)}, u32[]{:S(2)}) collective-permute-start(bf16[1,3,64,1024]{3,2,1,0:T(8,128)(2,1)S(1)} %get-tuple-element.9), channel_id=1, source_target_pairs={{16,0},{17,1},{18,2},{19,3},{20,4},{21,5},{22,6},{23,7},{24,8},{25... | collective-permute-start | bytes 1179656 | tf_op jit(solution)/shard_map/ppermute | solution.py:20
  168.8 0.7 copy-start.6
  168.8 0.7 copy-start.7
  168.8 0.7 copy-start.8
  168.8 243.5 %all-gather.11.cloned.1.call-start = ((), (), s32[]{:S(2)}) async-start(), calls=%async_computation.3 | async-start | bytes 37748736 | tf_op jit(solution)/shard_map/all_gather | solution.py:90
  250.8 3.4 copy-start.1
Sparse Core Ops, SparseCore 0:
  9.6 35.1 all-gather.4
  46.3 33.1 all-gather.6
  168.9 81.8 all-gather.8
  252.5 159.7 all-gather.10
where the time goes:
time: 463 us; the launch traced here: 462 us
  waiting for transfers between devices  311 us (67%)
  other arithmetic  68.8 us (15%)
  matrix products  55.3 us (12%)
  between operations  14 us (3%)
  local copies, waits for them, and re-layouts  9.49 us (2%)
    all_gather x1, waiting for transfers between devices, on_device(): lax.all_gather(expand_weight, ('seq', 'row'), axis=0, tiled=True)  157 us
    all_gather x1, waiting for transfers between devices, on_device(): gathered = lax.all_gather(flat_rows, 'col', axis=1, tiled=True)  81.3 us
    convert_element_type x1, other arithmetic, on_device(): (convolved + depth_bias.astype(jnp.float32)).astype(jnp.bfloat16)  53.4 us
    dot_general x1, matrix products, on_device(): jnp.dot(normed, lax.all_gather(expand_weight, ('seq', 'row'), axis=0, til...  43.5 us
    all_gather x1, waiting for transfers between devices, on_device(): keys_in = lax.all_gather(key_proj, 'seq', axis=1, tiled=True)  35.7 us
    all_gather x1, waiting for transfers between devices, on_device(): values_in = lax.all_gather(value_proj, 'seq', axis=1, tiled=True)  25.2 us
  transfers between devices with their start and end apart: 6, of which 6 were waited for; matrix products, arithmetic and copies ran while one was open for 3% of the time, Pallas kernels for 0%

commit v1 on v0

--- a/solution.py
+++ b/solution.py
@@ -1,12 +1,16 @@
+import functools
 import math
 
 import jax
 import jax.numpy as jnp
 from jax import lax
+from jax.experimental import pallas as pl
+from jax.experimental.pallas import tpu as pltpu
 from jax.sharding import PartitionSpec as P
 
 HEAD_DIM = 128
 KERNEL = 7
+VMEM_BYTES = 62 * 1024 * 1024
 
 
 def padded_2(array, sides, width):
@@ -96,9 +100,388 @@
     return (residual_out, hidden.reshape(samples, rows_here, col_count, expand_weight.shape[1]))
 
 
+def whole_block(
+    x_ref, q_ref, k_ref, v_ref, taps_ref, dbias_ref, gain_ref, nbias_ref, w_ref, ebias_ref,
+    res_ref, out_ref,
+    k_in, v_in, halo, rows_f32, shifted, acts, weights, total,
+    kv_send, kv_recv, halo_send, halo_recv, z_send, z_recv, own_sem,
+    y_send, y_recv, x_send, x_recv, far_send, far_recv, core_send, core_recv,
+    *, heads, rows, width, planes,
+):
+    seq, row, col = (lax.axis_index(a) for a in ("seq", "row", "col"))
+    positions = rows * width
+    margin = KERNEL // 2
+    strip = margin * width
+    chans = heads * HEAD_DIM
+    depth = w_ref.shape[0]
+    pieces, piece = total.shape[0], total.shape[2]
+    to_x = {"seq": 1 - seq}
+    to_y = {"row": lax.rem(row + 2, 4)}
+    to_core = {"row": row + 1 - 2 * lax.rem(row, 2)}
+    z_peers = [{"col": lax.rem(col + i, planes)} for i in range(1, planes)]
+
+    def remote(src, dst, send, recv, where):
+        return pltpu.make_async_remote_copy(
+            src_ref=src, dst_ref=dst, send_sem=send, recv_sem=recv,
+            device_id=where, device_id_type=pl.DeviceIdType.MESH,
+        )
+
+    def lanes(h):
+        return pl.ds(pl.multiple_of(h * HEAD_DIM, HEAD_DIM), HEAD_DIM)
+
+    def key_copy(h):
+        return remote(k_ref.at[:, lanes(h)], k_in.at[h], kv_send.at[h], kv_recv.at[h], to_x)
+
+    def value_copy(h):
+        return remote(
+            v_ref.at[:, lanes(h)], v_in.at[h], kv_send.at[heads + h], kv_recv.at[heads + h], to_x
+        )
+
+    def halo_copy(h):
+        start = pl.multiple_of((1 - seq) * (positions - strip), width)
+        return remote(
+            res_ref.at[pl.ds(start, strip), lanes(h)], halo.at[h],
+            halo_send.at[h], halo_recv.at[h], to_x,
+        )
+
+    def act_lanes(h, plane):
+        return pl.ds(pl.multiple_of(plane * chans + h * HEAD_DIM, HEAD_DIM), HEAD_DIM)
+
+    def act_copy(h, i):
+        part = acts.at[:, act_lanes(h, col)]
+        return remote(
+            part, part, z_send.at[i * heads + h], z_recv.at[i * heads + h], z_peers[i]
+        )
+
+    def act_arrival(h, i):
+        plane = lax.rem(col + planes - i - 1, planes)
+        part = acts.at[:, act_lanes(h, plane)]
+        return remote(
+            part, part, z_send.at[i * heads + h], z_recv.at[i * heads + h], z_peers[i]
+        )
+
+    def own_piece(j):
+        return w_ref.at[:, pl.ds(j * piece, piece)]
+
+    def own_copy(j):
+        return pltpu.make_async_copy(own_piece(j), weights.at[0, j], own_sem.at[j])
+
+    def y_copy(j):
+        return remote(own_piece(j), weights.at[1, j], y_send.at[j], y_recv.at[j], to_y)
+
+    def x_copy(j):
+        return remote(own_piece(j), weights.at[2, j], x_send.at[j], x_recv.at[j], to_x)
+
+    def far_copy(j):
+        if j < pieces - 1:
+            return remote(
+                weights.at[2, j], weights.at[3, j], far_send.at[j], far_recv.at[j], to_y
+            )
+        return remote(weights.at[1, j], weights.at[3, j], far_send.at[j], far_recv.at[j], to_x)
+
+    def core_copy(b, j):
+        src = own_piece(j) if b == 0 else weights.at[b, j]
+        at = b * pieces + j
+        return remote(src, weights.at[4 + b, j], core_send.at[at], core_recv.at[at], to_core)
+
+    barrier = pltpu.get_barrier_semaphore()
+    peers = [to_x, to_y, to_core] + z_peers
+    for peer in peers:
+        pl.semaphore_signal(
+            barrier, inc=1, device_id=peer, device_id_type=pl.DeviceIdType.MESH
+        )
+    pl.semaphore_wait(barrier, len(peers))
+
+    @pl.loop(0, heads)
+    def _(h):
+        key_copy(h).start()
+        value_copy(h).start()
+
+    for j in range(pieces):
+        y_copy(j).start()
+    for j in range(pieces):
+        own_copy(j).start()
+        core_copy(0, j).start()
+
+    scale = 1.0 / math.sqrt(HEAD_DIM)
+    half = positions // 2
+    shifted[...] = jnp.zeros_like(shifted)
+
+    def attend(h):
+        keys, values = k_ref[:, lanes(h)], v_ref[:, lanes(h)]
+        far_keys, far_values = k_in[h], v_in[h]
+        over = (((1,), (1,)), ((), ()))
+
+        @pl.loop(0, 2)
+        def _(i):
+            here = pl.ds(pl.multiple_of(i * half, half), half)
+            queries = q_ref[here, lanes(h)]
+            near = lax.dot_general(queries, keys, over, preferred_element_type=jnp.float32) * scale
+            far = lax.dot_general(queries, far_keys, over, preferred_element_type=jnp.float32) * scale
+            peak = jnp.maximum(
+                jnp.max(near, axis=1, keepdims=True), jnp.max(far, axis=1, keepdims=True)
+            )
+            near, far = jnp.exp(near - peak), jnp.exp(far - peak)
+            count = jnp.sum(near, axis=1, keepdims=True) + jnp.sum(far, axis=1, keepdims=True)
+            mixed = jnp.dot(
+                near.astype(jnp.bfloat16), values, preferred_element_type=jnp.float32
+            ) + jnp.dot(far.astype(jnp.bfloat16), far_values, preferred_element_type=jnp.float32)
+            res_ref[here, lanes(h)] = (
+                x_ref[here, lanes(h)].astype(jnp.float32) + mixed / count
+            ).astype(jnp.bfloat16)
+
+    def convolve(h):
+        edge = halo[h].astype(jnp.float32)
+        lead, trail = margin * width, (margin + rows) * width
+        rows_f32[0:lead, :] = jnp.where(seq == 1, edge, 0.0)
+        rows_f32[lead:trail, :] = res_ref[:, lanes(h)].astype(jnp.float32)
+        rows_f32[trail:, :] = jnp.where(seq == 0, edge, 0.0)
+        group = 4
+
+        @pl.loop(0, rows // group)
+        def _(g):
+            base = g * (group * width)
+            for q in range(KERNEL):
+                sums = [None] * group
+                for r in range(group + KERNEL - 1):
+                    start = pl.multiple_of(base + r * width, width)
+                    line = rows_f32[pl.ds(start, width), :]
+                    for o in range(group):
+                        p = r - o
+                        if 0 <= p < KERNEL:
+                            term = line * taps_ref[pl.ds(p * KERNEL + q, 1), lanes(h)]
+                            sums[o] = term if sums[o] is None else sums[o] + term
+                for o in range(group):
+                    shifted[o, q, 8 : 8 + width, :] = sums[o]
+            for o in range(group):
+                value = shifted[o, margin, 8 : 8 + width, :] + dbias_ref[:, lanes(h)]
+                for q in range(KERNEL):
+                    if q != margin:
+                        begin = 8 + q - margin
+                        value = value + shifted[o, q, begin : begin + width, :]
+                start = pl.multiple_of(base + o * width, width)
+                acts[pl.ds(start, width), act_lanes(h, col)] = value.astype(jnp.bfloat16)
+
+    @pl.loop(0, heads + 1)
+    def _(h):
+        @pl.when(h < heads)
+        def _():
+            key_copy(h).wait_recv()
+            value_copy(h).wait_recv()
+
+            @pl.when(h == heads - 1)
+            def _():
+                x_copy(0).start()
+
+            attend(h)
+            halo_copy(h).start()
+
+        @pl.when(h == heads)
+        def _():
+            for j in range(1, pieces):
+                x_copy(j).start()
+
+        @pl.when(h > 0)
+        def _():
+            halo_copy(h - 1).wait_recv()
+            convolve(h - 1)
+            for i in range(planes - 1):
+                act_copy(h - 1, i).start()
+
+    def y_arrived(j):
+        y_copy(j).wait_recv()
+        core_copy(1, j).start()
+        if j == pieces - 1:
+            far_copy(j).start()
+
+    def x_arrived(j):
+        x_copy(j).wait_recv()
+        if j < pieces - 1:
+            far_copy(j).start()
+        core_copy(2, j).start()
+
+    def far_arrived(j):
+        far_copy(j).wait_recv()
+        core_copy(3, j).start()
+
+    y_arrived(0)
+    y_arrived(1)
+    x_arrived(0)
+    y_arrived(2)
+    x_arrived(1)
+    y_arrived(3)
+
+    @pl.loop(0, heads)
+    def _(h):
+        for i in range(planes - 1):
+            act_arrival(h, i).wait_recv()
+            act_copy(h, i).wait_send()
+
+    x_arrived(2)
+    block = 16
+    inverse = 1.0 / acts.shape[1]
+
+    @pl.loop(0, positions // block)
+    def _(i):
+        here = pl.ds(pl.multiple_of(i * block, block), block)
+        wide = acts[here, :].astype(jnp.float32)
+        center = jnp.sum(wide, axis=1, keepdims=True) * inverse
+        wide = wide - center
+        spread = jnp.sum(wide * wide, axis=1, keepdims=True) * inverse
+        acts[here, :] = (
+            wide * lax.rsqrt(spread + 1e-06) * gain_ref[...] + nbias_ref[...]
+        ).astype(jnp.bfloat16)
+
+    other = row + 1 - 2 * lax.rem(row, 2)
+    places = []
+    for r in (row, other):
+        y = lax.rem(r + 2, 4)
+        places.append([seq * 4 + r, seq * 4 + y, (1 - seq) * 4 + r, (1 - seq) * 4 + y])
+    places = places[0] + places[1]
+
+    def product(here, j, slots):
+        result = None
+        for slot in slots:
+            cols = pl.ds(pl.multiple_of(places[slot] * depth, depth), depth)
+            term = jnp.dot(
+                acts[here, cols], weights[slot, j], preferred_element_type=jnp.float32
+            )
+            result = term if result is None else result + term
+        return result
+
+    tile = 256
+
+    def first(j):
+        @pl.loop(0, positions // tile)
+        def _(i):
+            here = pl.ds(pl.multiple_of(i * tile, tile), tile)
+            total[j, here, :] = product(here, j, (0, 4, 1, 5))
+
+    def second(j):
+        core_copy(2, j).wait_recv()
+
+        @pl.loop(0, positions // tile)
+        def _(i):
+            here = pl.ds(pl.multiple_of(i * tile, tile), tile)
+            total[j, here, :] += product(here, j, (2, 6))
+
+    def third(j):
+        core_copy(3, j).wait_recv()
+        cols = slice(j * piece, (j + 1) * piece)
+
+        @pl.loop(0, positions // tile)
+        def _(i):
+            here = pl.ds(pl.multiple_of(i * tile, tile), tile)
+            value = total[j, here, :] + product(here, j, (3, 7)) + ebias_ref[:, cols]
+            out_ref[here, cols] = (
+                0.5 * value * (1.0 + lax.erf(value * (1.0 / math.sqrt(2.0))))
+            ).astype(jnp.bfloat16)
+
+    for j in range(pieces):
+        own_copy(j).wait()
+        core_copy(0, j).wait_recv()
+        core_copy(1, j).wait_recv()
+    first(0)
+    first(1)
+    x_arrived(3)
+    far_arrived(0)
+    first(2)
+    first(3)
+    for j in range(pieces):
+        second(j)
+    far_arrived(1)
+    third(0)
+    far_arrived(2)
+    third(1)
+    far_arrived(3)
+    third(2)
+    third(3)
+
+    @pl.loop(0, heads)
+    def _(h):
+        key_copy(h).wait_send()
+        value_copy(h).wait_send()
+        halo_copy(h).wait_send()
+
+    for j in range(pieces):
+        y_copy(j).wait_send()
+        x_copy(j).wait_send()
+        far_copy(j).wait_send()
+        for b in range(4):
+            core_copy(b, j).wait_send()
+
+
+def on_device_kernel(
+    planes,
+    inputs,
+    query_proj,
+    key_proj,
+    value_proj,
+    depth_weight,
+    depth_bias,
+    norm_gain,
+    norm_bias,
+    expand_weight,
+    expand_bias,
+):
+    _, rows, width, chans = inputs.shape
+    positions, heads = rows * width, chans // HEAD_DIM
+    depth, units = expand_weight.shape
+    pieces = 4
+    piece = units // pieces
+    margin = KERNEL // 2
+
+    def flat(array):
+        return array.reshape(positions, chans)
+
+    def wide(array, lead=1):
+        return array.astype(jnp.float32).reshape(lead, -1)
+
+    vmem, anywhere = pl.BlockSpec(memory_space=pltpu.VMEM), pl.BlockSpec(memory_space=pl.ANY)
+    dma = pltpu.SemaphoreType.DMA
+    residual, hidden = pl.pallas_call(
+        functools.partial(whole_block, heads=heads, rows=rows, width=width, planes=planes),
+        out_shape=(
+            jax.ShapeDtypeStruct((positions, chans), jnp.bfloat16),
+            jax.ShapeDtypeStruct((positions, units), jnp.bfloat16),
+        ),
+        in_specs=[vmem] * 8 + [anywhere, vmem],
+        out_specs=(vmem, vmem),
+        scratch_shapes=[
+            pltpu.VMEM((heads, positions, HEAD_DIM), jnp.bfloat16),
+            pltpu.VMEM((heads, positions, HEAD_DIM), jnp.bfloat16),
+            pltpu.VMEM((heads, margin * width, HEAD_DIM), jnp.bfloat16),
+            pltpu.VMEM(((rows + 2 * margin) * width, HEAD_DIM), jnp.float32),
+            pltpu.VMEM((4, KERNEL, width + 16, HEAD_DIM), jnp.float32),
+            pltpu.VMEM((positions, planes * chans), jnp.bfloat16),
+            pltpu.VMEM((8, pieces, depth, piece), jnp.bfloat16),
+            pltpu.VMEM((pieces, positions, piece), jnp.float32),
+            dma((2 * heads,)), dma((2 * heads,)),
+            dma((heads,)), dma((heads,)),
+            dma(((planes - 1) * heads,)), dma(((planes - 1) * heads,)),
+            dma((pieces,)),
+            dma((pieces,)), dma((pieces,)),
+            dma((pieces,)), dma((pieces,)),
+            dma((pieces,)), dma((pieces,)),
+            dma((4 * pieces,)), dma((4 * pieces,)),
+        ],
+        compiler_params=pltpu.CompilerParams(
+            collective_id=0, has_side_effects=True, vmem_limit_bytes=VMEM_BYTES
+        ),
+    )(
+        flat(inputs), flat(query_proj), flat(key_proj), flat(value_proj),
+        wide(depth_weight, KERNEL * KERNEL), wide(depth_bias), wide(norm_gain), wide(norm_bias),
+        expand_weight, wide(expand_bias),
+    )
+    return (residual.reshape(inputs.shape), hidden.reshape(1, rows, width, units))
+
+
 def solution(mesh):
+    body = on_device
+    if mesh.shape["seq"] == 2 and mesh.shape["row"] == 4:
+        body = functools.partial(on_device_kernel, mesh.shape["col"])
     return jax.shard_map(
-        on_device,
+        body,
         mesh=mesh,
         in_specs=(
             P("row", "seq", None, "col"),

time: 463 us -> 206 us (0.44)
  waiting for transfers between devices: 311 us -> 0 us
  Pallas kernels: 0 us -> 191 us
  other arithmetic: 68.8 us -> 5.18 us
  matrix products: 55.3 us -> 0 us
  between operations: 14 us -> 0.64 us
    all_gather x4 -> x0, waiting for transfers between devices: 299 us -> none  [the longest x1 157 us: on_device(): lax.all_gather(expand_weight, ('seq', 'row'), axis=0, tiled=True)]
    pallas_call x0 -> x1, Pallas kernels: none -> 191 us  [on_device_kernel(): pl.pallas_call(functools.partial(whole_block, heads=heads, rows=rows, wid...]
    convert_element_type x7 -> x0, other arithmetic: 56.8 us -> none  [the longest x1 53.4 us: on_device(): (convolved + depth_bias.astype(jnp.float32)).astype(jnp.bfloat16)]
    dot_general x3 -> x0, matrix products: 55.3 us -> none  [the longest x1 43.5 us: on_device(): jnp.dot(normed, lax.all_gather(expand_weight, ('seq', 'row'), axis=0, til...]
    reduce_sum x3 -> x0, other arithmetic: 12 us -> none  [the longest x1 7.84 us: on_device(): new_total = jnp.sum(weights, axis=-1)]
    ppermute x2 -> x0, waiting for transfers between devices: 10.2 us -> none  [the longest x1 6.34 us: padded_2(): before = lax.ppermute(last, axis, up)]
    reshape x0 -> x4, other arithmetic: none -> 5.18 us  [wide(): return array.astype(jnp.float32).reshape(lead, -1)]
  transfers between devices with their start and end apart: 6 -> 0, of which waited for: 6 -> 0; matrix products, arithmetic and copies ran while one was open for 3% -> 0% of each run, Pallas kernels for 0% -> 0%
where the time goes in v1:
time: 206 us
  Pallas kernels  191 us (93%)
  local copies, waits for them, and re-layouts  8.58 us (4%)
  other arithmetic  5.18 us (3%)
    pallas_call x1, Pallas kernels, on_device_kernel(): pl.pallas_call(functools.partial(whole_block, heads=heads, rows=rows, wid...  191 us
    unnamed x2, local copies, waits for them, and re-layouts  6.96 us
    reshape x4, other arithmetic, wide(): return array.astype(jnp.float32).reshape(lead, -1)  5.18 us

profile of v1, /device:TPU:1, one launch (start us, length us, event | category | flops | bytes accessed | tf_op | source)
XLA Modules:
  0.0 205.6 jit_solution(7994183275936454393)
XLA Ops:
  0.6 1.3 reshape.65
  1.9 1.3 reshape.67
  3.2 1.3 reshape.69
  4.5 1.3 reshape.71
  5.8 1.6 reshape.64.taps_ref
  7.4 191.2 %shard_map.113 = (bf16[512,1024]{1,0:T(8,128)(2,1)}, bf16[512,4096]{1,0:T(8,128)(2,1)}) custom-call(bf16[512,1024]{1,0:T(8,128)(2,1)} %bitcast.12, bf16[512,1024]{1,0:T(8,128)(2,1)} %bitcast.13, bf16[512,1024]{1,0:T(8,128)(2,1)} %bitcast.14, bf16[512,1024]{1,0:T(8,128)(2,1)} %bitcast.15, f32[49,1024]{1,0:T(8,128)} %reshape.64.taps_ref, f32[1,1024]{1,0:T(1,128)} %bitcast.19, ...), custom_call_target="tpu_custom_call" | custom-call | tf_op jit(solution)/shard_map/pallas_call | solution.py:442
  198.6 2.3 %copy.14 = bf16[1,8,64,1024]{3,2,1,0:T(8,128)(2,1)} copy(bf16[1,8,64,1024]{3,2,1,0:T(8,128)(2,1)} %bitcast.11) | data formatting | bytes 2097152
  200.9 4.7 %copy.15 = bf16[1,8,64,4096]{3,2,1,0:T(8,128)(2,1)} copy(bf16[1,8,64,4096]{3,2,1,0:T(8,128)(2,1)} %bitcast.10) | data formatting | bytes 8388608

commit v2 on v1

--- a/solution.py
+++ b/solution.py
@@ -101,9 +101,9 @@
 
 
 def whole_block(
-    x_ref, q_ref, k_ref, v_ref, taps_ref, dbias_ref, gain_ref, nbias_ref, w_ref, ebias_ref,
+    x_ref, q_ref, k_ref, v_ref, taps_ref, vectors_ref, w_ref,
     res_ref, out_ref,
-    k_in, v_in, halo, rows_f32, shifted, acts, weights, total,
+    k_in, v_in, halo, rows_f32, shifted, taps, acts, weights, total,
     kv_send, kv_recv, halo_send, halo_recv, z_send, z_recv, own_sem,
     y_send, y_recv, x_send, x_recv, far_send, far_recv, core_send, core_recv,
     *, heads, rows, width, planes,
@@ -115,6 +115,7 @@
     chans = heads * HEAD_DIM
     depth = w_ref.shape[0]
     pieces, piece = total.shape[0], total.shape[2]
+    by_y, ahead, lag = pieces * 3 // 4, 3, 2
     to_x = {"seq": 1 - seq}
     to_y = {"row": lax.rem(row + 2, 4)}
     to_core = {"row": row + 1 - 2 * lax.rem(row, 2)}
@@ -173,7 +174,7 @@
         return remote(own_piece(j), weights.at[2, j], x_send.at[j], x_recv.at[j], to_x)
 
     def far_copy(j):
-        if j < pieces - 1:
+        if j < by_y:
             return remote(
                 weights.at[2, j], weights.at[3, j], far_send.at[j], far_recv.at[j], to_y
             )
@@ -192,11 +193,9 @@
         )
     pl.semaphore_wait(barrier, len(peers))
 
-    @pl.loop(0, heads)
-    def _(h):
+    for h in range(min(ahead, heads)):
         key_copy(h).start()
         value_copy(h).start()
-
     for j in range(pieces):
         y_copy(j).start()
     for j in range(pieces):
@@ -206,6 +205,14 @@
     scale = 1.0 / math.sqrt(HEAD_DIM)
     half = positions // 2
     shifted[...] = jnp.zeros_like(shifted)
+    taps[...] = taps_ref[...].astype(jnp.float32)
+
+    channels = acts.shape[1]
+    gain_at, nbias_at = chans, chans + channels
+    ebias_at = nbias_at + channels
+
+    def vector(start, size):
+        return vectors_ref[:, pl.ds(start, size)]
 
     def attend(h):
         keys, values = k_ref[:, lanes(h)], v_ref[:, lanes(h)]
@@ -249,12 +256,12 @@
                     for o in range(group):
                         p = r - o
                         if 0 <= p < KERNEL:
-                            term = line * taps_ref[pl.ds(p * KERNEL + q, 1), lanes(h)]
+                            term = line * taps[p, q : q + 1, lanes(h)]
                             sums[o] = term if sums[o] is None else sums[o] + term
                 for o in range(group):
                     shifted[o, q, 8 : 8 + width, :] = sums[o]
             for o in range(group):
-                value = shifted[o, margin, 8 : 8 + width, :] + dbias_ref[:, lanes(h)]
+                value = shifted[o, margin, 8 : 8 + width, :] + vectors_ref[:, lanes(h)]
                 for q in range(KERNEL):
                     if q != margin:
                         begin = 8 + q - margin
@@ -262,54 +269,61 @@
                 start = pl.multiple_of(base + o * width, width)
                 acts[pl.ds(start, width), act_lanes(h, col)] = value.astype(jnp.bfloat16)
 
-    @pl.loop(0, heads + 1)
+    def y_arrived(j):
+        y_copy(j).wait_recv()
+        core_copy(1, j).start()
+        if j >= by_y:
+            far_copy(j).start()
+
+    def x_arrived(j):
+        x_copy(j).wait_recv()
+        if j < by_y:
+            far_copy(j).start()
+        core_copy(2, j).start()
+
+    def far_arrived(j):
+        far_copy(j).wait_recv()
+        core_copy(3, j).start()
+
+    @pl.loop(0, heads + lag)
     def _(h):
+        @pl.when(h + ahead < heads)
+        def _():
+            key_copy(h + ahead).start()
+            value_copy(h + ahead).start()
+
+        for j, when in enumerate((2, 4, 6)):
+            @pl.when(h == when)
+            def _():
+                x_copy(j).start()
+
         @pl.when(h < heads)
         def _():
             key_copy(h).wait_recv()
             value_copy(h).wait_recv()
-
-            @pl.when(h == heads - 1)
-            def _():
-                x_copy(0).start()
-
             attend(h)
             halo_copy(h).start()
 
         @pl.when(h == heads)
         def _():
-            for j in range(1, pieces):
+            for j in range(3, pieces):
                 x_copy(j).start()
-
-        @pl.when(h > 0)
+            for j in range(pieces):
+                y_arrived(j)
+            x_arrived(0)
+
+        @pl.when(h == heads + 1)
         def _():
-            halo_copy(h - 1).wait_recv()
-            convolve(h - 1)
+            x_arrived(1)
+
+        @pl.when(h >= lag)
+        def _():
+            halo_copy(h - lag).wait_recv()
+            convolve(h - lag)
             for i in range(planes - 1):
-                act_copy(h - 1, i).start()
-
-    def y_arrived(j):
-        y_copy(j).wait_recv()
-        core_copy(1, j).start()
-        if j == pieces - 1:
-            far_copy(j).start()
-
-    def x_arrived(j):
-        x_copy(j).wait_recv()
-        if j < pieces - 1:
-            far_copy(j).start()
-        core_copy(2, j).start()
-
-    def far_arrived(j):
-        far_copy(j).wait_recv()
-        core_copy(3, j).start()
-
-    y_arrived(0)
-    y_arrived(1)
-    x_arrived(0)
-    y_arrived(2)
-    x_arrived(1)
-    y_arrived(3)
+                act_copy(h - lag, i).start()
+
+    x_arrived(2)
 
     @pl.loop(0, heads)
     def _(h):
@@ -317,7 +331,7 @@
             act_arrival(h, i).wait_recv()
             act_copy(h, i).wait_send()
 
-    x_arrived(2)
+    x_arrived(3)
     block = 16
     inverse = 1.0 / acts.shape[1]
 
@@ -329,7 +343,7 @@
         wide = wide - center
         spread = jnp.sum(wide * wide, axis=1, keepdims=True) * inverse
         acts[here, :] = (
-            wide * lax.rsqrt(spread + 1e-06) * gain_ref[...] + nbias_ref[...]
+            wide * lax.rsqrt(spread + 1e-06) * vector(gain_at, channels) + vector(nbias_at, channels)
         ).astype(jnp.bfloat16)
 
     other = row + 1 - 2 * lax.rem(row, 2)
@@ -372,7 +386,7 @@
         @pl.loop(0, positions // tile)
         def _(i):
             here = pl.ds(pl.multiple_of(i * tile, tile), tile)
-            value = total[j, here, :] + product(here, j, (3, 7)) + ebias_ref[:, cols]
+            value = total[j, here, :] + product(here, j, (3, 7)) + vector(ebias_at + j * piece, piece)
             out_ref[here, cols] = (
                 0.5 * value * (1.0 + lax.erf(value * (1.0 / math.sqrt(2.0))))
             ).astype(jnp.bfloat16)
@@ -381,21 +395,26 @@
         own_copy(j).wait()
         core_copy(0, j).wait_recv()
         core_copy(1, j).wait_recv()
-    first(0)
-    first(1)
-    x_arrived(3)
+    for j in range(4):
+        first(j)
+    x_arrived(4)
+    x_arrived(5)
     far_arrived(0)
-    first(2)
-    first(3)
-    for j in range(pieces):
+    for j in range(4, pieces):
+        first(j)
+    x_arrived(6)
+    far_arrived(1)
+    for j in range(4):
         second(j)
-    far_arrived(1)
-    third(0)
     far_arrived(2)
-    third(1)
-    far_arrived(3)
-    third(2)
-    third(3)
+    x_arrived(7)
+    for j in range(4, pieces):
+        second(j)
+    for j in range(3, pieces):
+        far_arrived(j)
+        third(j - 3)
+    for j in range(pieces - 3, pieces):
+        third(j)
 
     @pl.loop(0, heads)
     def _(h):
@@ -427,16 +446,15 @@
     _, rows, width, chans = inputs.shape
     positions, heads = rows * width, chans // HEAD_DIM
     depth, units = expand_weight.shape
-    pieces = 4
+    pieces = 8
     piece = units // pieces
     margin = KERNEL // 2
 
     def flat(array):
         return array.reshape(positions, chans)
 
-    def wide(array, lead=1):
-        return array.astype(jnp.float32).reshape(lead, -1)
-
+    vectors = jnp.concatenate([depth_bias, norm_gain, norm_bias, expand_bias])
+    vectors = lax.optimization_barrier(vectors.astype(jnp.float32)).reshape(1, -1)
     vmem, anywhere = pl.BlockSpec(memory_space=pltpu.VMEM), pl.BlockSpec(memory_space=pl.ANY)
     dma = pltpu.SemaphoreType.DMA
     residual, hidden = pl.pallas_call(
@@ -445,7 +463,7 @@
             jax.ShapeDtypeStruct((positions, chans), jnp.bfloat16),
             jax.ShapeDtypeStruct((positions, units), jnp.bfloat16),
         ),
-        in_specs=[vmem] * 8 + [anywhere, vmem],
+        in_specs=[vmem] * 6 + [anywhere],
         out_specs=(vmem, vmem),
         scratch_shapes=[
             pltpu.VMEM((heads, positions, HEAD_DIM), jnp.bfloat16),
@@ -453,6 +471,7 @@
             pltpu.VMEM((heads, margin * width, HEAD_DIM), jnp.bfloat16),
             pltpu.VMEM(((rows + 2 * margin) * width, HEAD_DIM), jnp.float32),
             pltpu.VMEM((4, KERNEL, width + 16, HEAD_DIM), jnp.float32),
+            pltpu.VMEM((KERNEL, KERNEL, chans), jnp.float32),
             pltpu.VMEM((positions, planes * chans), jnp.bfloat16),
             pltpu.VMEM((8, pieces, depth, piece), jnp.bfloat16),
             pltpu.VMEM((pieces, positions, piece), jnp.float32),
@@ -470,8 +489,7 @@
         ),
     )(
         flat(inputs), flat(query_proj), flat(key_proj), flat(value_proj),
-        wide(depth_weight, KERNEL * KERNEL), wide(depth_bias), wide(norm_gain), wide(norm_bias),
-        expand_weight, wide(expand_bias),
+        depth_weight, vectors, expand_weight,
     )
     return (residual.reshape(inputs.shape), hidden.reshape(1, rows, width, units))
 

time: 206 us -> 192 us (0.932)
  Pallas kernels: 191 us -> 182 us
  other arithmetic: 5.18 us -> 1.36 us
    pallas_call x1, Pallas kernels: 191 us -> 182 us  [on_device_kernel(): pl.pallas_call(functools.partial(whole_block, heads=heads, rows=rows, wid...]
    reshape x4 -> x0, other arithmetic: 5.18 us -> none  [wide(): return array.astype(jnp.float32).reshape(lead, -1)]
where the time goes in v2:
time: 192 us; the launch traced here: 191 us
  Pallas kernels  182 us (95%)
  local copies, waits for them, and re-layouts  6.96 us (4%)
    pallas_call x1, Pallas kernels, on_device_kernel(): pl.pallas_call(functools.partial(whole_block, heads=heads, rows=rows, wid...  182 us
    unnamed x2, local copies, waits for them, and re-layouts  6.96 us

profile of v2, /device:TPU:1, one launch (start us, length us, event | category | flops | bytes accessed | tf_op | source)
XLA Modules:
  0.0 190.7 jit_solution(16530504190207381951)
XLA Ops:
  0.6 1.4 maximum_convert_fusion
  2.0 181.7 %shard_map.113 = (bf16[512,1024]{1,0:T(8,128)(2,1)}, bf16[512,4096]{1,0:T(8,128)(2,1)}) custom-call(bf16[512,1024]{1,0:T(8,128)(2,1)} %bitcast.9, bf16[512,1024]{1,0:T(8,128)(2,1)} %bitcast.10, bf16[512,1024]{1,0:T(8,128)(2,1)} %bitcast.11, bf16[512,1024]{1,0:T(8,128)(2,1)} %bitcast.12, bf16[7,7,1024]{2,1,0:T(8,128)(2,1)} %taps_ref.1, f32[1,13312]{1,0:T(1,128)} %bitcast.13, ...), custom_call_target="tpu_custom_call" | custom-call | tf_op jit(solution)/shard_map/pallas_call | solution.py:460
  183.7 2.3 %copy.14 = bf16[1,8,64,1024]{3,2,1,0:T(8,128)(2,1)} copy(bf16[1,8,64,1024]{3,2,1,0:T(8,128)(2,1)} %bitcast.8) | data formatting | bytes 2097152
  186.0 4.7 %copy.15 = bf16[1,8,64,4096]{3,2,1,0:T(8,128)(2,1)} copy(bf16[1,8,64,4096]{3,2,1,0:T(8,128)(2,1)} %bitcast.7) | data formatting | bytes 8388608

commit v3 on v2

--- a/solution.py
+++ b/solution.py
@@ -10,6 +10,7 @@
 
 HEAD_DIM = 128
 KERNEL = 7
+COPY_PARTS = 8
 VMEM_BYTES = 62 * 1024 * 1024
 
 
@@ -101,10 +102,11 @@
 
 
 def whole_block(
-    x_ref, q_ref, k_ref, v_ref, taps_ref, vectors_ref, w_ref,
-    res_ref, out_ref,
+    x_hbm, q_hbm, k_hbm, v_hbm, taps_ref, vectors_ref, w_ref,
+    res_hbm, out_hbm,
+    x_ref, q_ref, k_ref, v_ref, res_ref, out_ref,
     k_in, v_in, halo, rows_f32, shifted, taps, acts, weights, total,
-    kv_send, kv_recv, halo_send, halo_recv, z_send, z_recv, own_sem,
+    in_sem, res_sem, out_sem, kv_send, kv_recv, halo_send, halo_recv, z_send, z_recv, own_sem,
     y_send, y_recv, x_send, x_recv, far_send, far_recv, core_send, core_recv,
     *, heads, rows, width, planes,
 ):
@@ -131,11 +133,11 @@
         return pl.ds(pl.multiple_of(h * HEAD_DIM, HEAD_DIM), HEAD_DIM)
 
     def key_copy(h):
-        return remote(k_ref.at[:, lanes(h)], k_in.at[h], kv_send.at[h], kv_recv.at[h], to_x)
+        return remote(k_hbm.at[:, lanes(h)], k_in.at[h], kv_send.at[h], kv_recv.at[h], to_x)
 
     def value_copy(h):
         return remote(
-            v_ref.at[:, lanes(h)], v_in.at[h], kv_send.at[heads + h], kv_recv.at[heads + h], to_x
+            v_hbm.at[:, lanes(h)], v_in.at[h], kv_send.at[heads + h], kv_recv.at[heads + h], to_x
         )
 
     def halo_copy(h):
@@ -173,18 +175,42 @@
     def x_copy(j):
         return remote(own_piece(j), weights.at[2, j], x_send.at[j], x_recv.at[j], to_x)
 
-    def far_copy(j):
-        if j < by_y:
-            return remote(
-                weights.at[2, j], weights.at[3, j], far_send.at[j], far_recv.at[j], to_y
-            )
-        return remote(weights.at[1, j], weights.at[3, j], far_send.at[j], far_recv.at[j], to_x)
+    def far_part(j, rows_here, at, over_y):
+        src, where = (2, to_y) if over_y else (1, to_x)
+        return remote(
+            weights.at[src, j, rows_here], weights.at[3, j, rows_here],
+            far_send.at[at], far_recv.at[at], where,
+        )
+
+    def far_y(j):
+        if j == by_y:
+            return [far_part(j, pl.ds(0, depth // 2), j, True)]
+        return [far_part(j, pl.ds(0, depth), j, True)] if j < by_y else []
+
+    def far_x(j):
+        if j == by_y:
+            return [far_part(j, pl.ds(depth // 2, depth // 2), pieces, False)]
+        return [far_part(j, pl.ds(0, depth), j, False)] if j > by_y else []
 
     def core_copy(b, j):
         src = own_piece(j) if b == 0 else weights.at[b, j]
         at = b * pieces + j
         return remote(src, weights.at[4 + b, j], core_send.at[at], core_recv.at[at], to_core)
 
+    locals_in = [
+        pltpu.make_async_copy(src, dst, in_sem.at[i])
+        for i, (src, dst) in enumerate(
+            ((q_hbm, q_ref), (k_hbm, k_ref), (v_hbm, v_ref), (x_hbm, x_ref))
+        )
+    ]
+    res_copy = pltpu.make_async_copy(res_ref, res_hbm, res_sem.at[0])
+
+    def out_copy(j):
+        part = (slice(None), pl.ds(j * piece, piece))
+        return pltpu.make_async_copy(out_ref.at[part], out_hbm.at[part], out_sem.at[j])
+
+    for copy in locals_in:
+        copy.start()
     barrier = pltpu.get_barrier_semaphore()
     peers = [to_x, to_y, to_core] + z_peers
     for peer in peers:
@@ -207,6 +233,8 @@
     shifted[...] = jnp.zeros_like(shifted)
     taps[...] = taps_ref[...].astype(jnp.float32)
 
+    for copy in locals_in:
+        copy.wait()
     channels = acts.shape[1]
     gain_at, nbias_at = chans, chans + channels
     ebias_at = nbias_at + channels
@@ -272,17 +300,18 @@
     def y_arrived(j):
         y_copy(j).wait_recv()
         core_copy(1, j).start()
-        if j >= by_y:
-            far_copy(j).start()
+        for part in far_x(j):
+            part.start()
 
     def x_arrived(j):
         x_copy(j).wait_recv()
-        if j < by_y:
-            far_copy(j).start()
+        for part in far_y(j):
+            part.start()
         core_copy(2, j).start()
 
     def far_arrived(j):
-        far_copy(j).wait_recv()
+        for part in far_y(j) + far_x(j):
+            part.wait_recv()
         core_copy(3, j).start()
 
     @pl.loop(0, heads + lag)
@@ -308,13 +337,6 @@
         def _():
             for j in range(3, pieces):
                 x_copy(j).start()
-            for j in range(pieces):
-                y_arrived(j)
-            x_arrived(0)
-
-        @pl.when(h == heads + 1)
-        def _():
-            x_arrived(1)
 
         @pl.when(h >= lag)
         def _():
@@ -323,7 +345,15 @@
             for i in range(planes - 1):
                 act_copy(h - lag, i).start()
 
+    res_copy.start()
+    for j in range(5):
+        y_arrived(j)
+    x_arrived(0)
+    y_arrived(5)
+    x_arrived(1)
+    y_arrived(6)
     x_arrived(2)
+    y_arrived(7)
 
     @pl.loop(0, heads)
     def _(h):
@@ -390,6 +420,8 @@
             out_ref[here, cols] = (
                 0.5 * value * (1.0 + lax.erf(value * (1.0 / math.sqrt(2.0))))
             ).astype(jnp.bfloat16)
+
+        out_copy(j).start()
 
     for j in range(pieces):
         own_copy(j).wait()
@@ -410,11 +442,13 @@
     x_arrived(7)
     for j in range(4, pieces):
         second(j)
+    third(0)
+    third(1)
     for j in range(3, pieces):
         far_arrived(j)
-        third(j - 3)
-    for j in range(pieces - 3, pieces):
-        third(j)
+        third(j - 1)
+    third(pieces - 1)
+    res_copy.wait()
 
     @pl.loop(0, heads)
     def _(h):
@@ -425,9 +459,26 @@
     for j in range(pieces):
         y_copy(j).wait_send()
         x_copy(j).wait_send()
-        far_copy(j).wait_send()
+        for part in far_y(j) + far_x(j):
+            part.wait_send()
+        out_copy(j).wait()
         for b in range(4):
             core_copy(b, j).wait_send()
+
+
+def copy_out(res_in, out_in, res_ref, out_ref, sem):
+    copies = []
+    for i, (src, dst) in enumerate(((out_in, out_ref), (res_in, res_ref))):
+        size = src.shape[0] // COPY_PARTS
+        for n in range(COPY_PARTS):
+            part = pl.ds(n * size, size)
+            copies.append(
+                pltpu.make_async_copy(src.at[part], dst.at[part], sem.at[i * COPY_PARTS + n])
+            )
+    for copy in copies:
+        copy.start()
+    for copy in copies:
+        copy.wait()
 
 
 def on_device_kernel(
@@ -463,9 +514,11 @@
             jax.ShapeDtypeStruct((positions, chans), jnp.bfloat16),
             jax.ShapeDtypeStruct((positions, units), jnp.bfloat16),
         ),
-        in_specs=[vmem] * 6 + [anywhere],
-        out_specs=(vmem, vmem),
+        in_specs=[anywhere] * 4 + [vmem] * 2 + [anywhere],
+        out_specs=(anywhere, anywhere),
         scratch_shapes=[
+            *[pltpu.VMEM((positions, chans), jnp.bfloat16)] * 5,
+            pltpu.VMEM((positions, units), jnp.bfloat16),
             pltpu.VMEM((heads, positions, HEAD_DIM), jnp.bfloat16),
             pltpu.VMEM((heads, positions, HEAD_DIM), jnp.bfloat16),
             pltpu.VMEM((heads, margin * width, HEAD_DIM), jnp.bfloat16),
@@ -475,13 +528,14 @@
             pltpu.VMEM((positions, planes * chans), jnp.bfloat16),
             pltpu.VMEM((8, pieces, depth, piece), jnp.bfloat16),
             pltpu.VMEM((pieces, positions, piece), jnp.float32),
+            dma((4,)), dma((1,)), dma((pieces,)),
             dma((2 * heads,)), dma((2 * heads,)),
             dma((heads,)), dma((heads,)),
             dma(((planes - 1) * heads,)), dma(((planes - 1) * heads,)),
             dma((pieces,)),
             dma((pieces,)), dma((pieces,)),
             dma((pieces,)), dma((pieces,)),
-            dma((pieces,)), dma((pieces,)),
+            dma((pieces + 1,)), dma((pieces + 1,)),
             dma((4 * pieces,)), dma((4 * pieces,)),
         ],
         compiler_params=pltpu.CompilerParams(
@@ -491,6 +545,17 @@
         flat(inputs), flat(query_proj), flat(key_proj), flat(value_proj),
         depth_weight, vectors, expand_weight,
     )
+    residual, hidden = pl.pallas_call(
+        copy_out,
+        out_shape=(
+            jax.ShapeDtypeStruct((positions, chans), jnp.bfloat16),
+            jax.ShapeDtypeStruct((positions, units), jnp.bfloat16),
+        ),
+        in_specs=[anywhere] * 2,
+        out_specs=(anywhere, anywhere),
+        scratch_shapes=[dma((2 * COPY_PARTS,))],
+        compiler_params=pltpu.CompilerParams(vmem_limit_bytes=VMEM_BYTES),
+    )(residual, hidden)
     return (residual.reshape(inputs.shape), hidden.reshape(1, rows, width, units))
 
 

time: 192 us -> 340 us (1.77)
  Pallas kernels: 182 us -> 338 us
  local copies, waits for them, and re-layouts: 6.96 us -> 0 us
    pallas_call x0 -> x1, Pallas kernels: none -> 160 us  [on_device_kernel(): pl.pallas_call(copy_out, out_shape=(jax.ShapeDtypeStruct((positions, chan...]
    unnamed x2 -> x0, local copies, waits for them, and re-layouts: 6.96 us -> none
    pallas_call x1, Pallas kernels: 182 us -> 177 us  [on_device_kernel(): pl.pallas_call(functools.partial(whole_block, heads=heads, rows=rows, wid...]
where the time goes in v3:
time: 340 us
  Pallas kernels  338 us (99%)
    pallas_call x1, Pallas kernels, on_device_kernel(): pl.pallas_call(functools.partial(whole_block, heads=heads, rows=rows, wid...  177 us
    pallas_call x1, Pallas kernels, on_device_kernel(): pl.pallas_call(copy_out, out_shape=(jax.ShapeDtypeStruct((positions, chan...  160 us

profile of v3, /device:TPU:1, one launch (start us, length us, event | category | flops | bytes accessed | tf_op | source)
XLA Modules:
  0.0 339.5 jit_solution(12607754526464509005)
XLA Ops:
  0.6 1.4 maximum_convert_fusion
  2.0 177.4 %shard_map.113 = (bf16[512,1024]{1,0:T(8,128)(2,1)}, bf16[512,4096]{1,0:T(8,128)(2,1)}) custom-call(bf16[512,1024]{1,0:T(8,128)(2,1)} %bitcast.7, bf16[512,1024]{1,0:T(8,128)(2,1)} %bitcast.8, bf16[512,1024]{1,0:T(8,128)(2,1)} %bitcast.9, bf16[512,1024]{1,0:T(8,128)(2,1)} %bitcast.10, bf16[7,7,1024]{2,1,0:T(8,128)(2,1)} %taps_ref.1, f32[1,13312]{1,0:T(1,128)} %bitcast.11, ...), custom_call_target="tpu_custom_call" | custom-call | tf_op jit(solution)/shard_map/pallas_call | solution.py:511
  179.4 160.1 %shard_map.114 = (bf16[512,1024]{1,0:T(8,128)(2,1)}, bf16[512,4096]{1,0:T(8,128)(2,1)}) custom-call(bf16[512,1024]{1,0:T(8,128)(2,1)} %get-tuple-element.6.res_in, bf16[512,4096]{1,0:T(8,128)(2,1)} %get-tuple-element.7.out_in), custom_call_target="tpu_custom_call" | custom-call | tf_op jit(solution)/shard_map/pallas_call | solution.py:548

commit v4 on v3

--- a/solution.py
+++ b/solution.py
@@ -170,10 +170,10 @@
         return pltpu.make_async_copy(own_piece(j), weights.at[0, j], own_sem.at[j])
 
     def y_copy(j):
-        return remote(own_piece(j), weights.at[1, j], y_send.at[j], y_recv.at[j], to_y)
+        return remote(weights.at[0, j], weights.at[1, j], y_send.at[j], y_recv.at[j], to_y)
 
     def x_copy(j):
-        return remote(own_piece(j), weights.at[2, j], x_send.at[j], x_recv.at[j], to_x)
+        return remote(weights.at[0, j], weights.at[2, j], x_send.at[j], x_recv.at[j], to_x)
 
     def far_part(j, rows_here, at, over_y):
         src, where = (2, to_y) if over_y else (1, to_x)
@@ -193,9 +193,8 @@
         return [far_part(j, pl.ds(0, depth), j, False)] if j > by_y else []
 
     def core_copy(b, j):
-        src = own_piece(j) if b == 0 else weights.at[b, j]
         at = b * pieces + j
-        return remote(src, weights.at[4 + b, j], core_send.at[at], core_recv.at[at], to_core)
+        return remote(weights.at[b, j], weights.at[4 + b, j], core_send.at[at], core_recv.at[at], to_core)
 
     locals_in = [
         pltpu.make_async_copy(src, dst, in_sem.at[i])
@@ -211,6 +210,8 @@
 
     for copy in locals_in:
         copy.start()
+    for j in range(pieces):
+        own_copy(j).start()
     barrier = pltpu.get_barrier_semaphore()
     peers = [to_x, to_y, to_core] + z_peers
     for peer in peers:
@@ -223,9 +224,8 @@
         key_copy(h).start()
         value_copy(h).start()
     for j in range(pieces):
+        own_copy(j).wait()
         y_copy(j).start()
-    for j in range(pieces):
-        own_copy(j).start()
         core_copy(0, j).start()
 
     scale = 1.0 / math.sqrt(HEAD_DIM)
@@ -354,6 +354,8 @@
     y_arrived(6)
     x_arrived(2)
     y_arrived(7)
+    x_arrived(3)
+    x_arrived(4)
 
     @pl.loop(0, heads)
     def _(h):
@@ -361,7 +363,6 @@
             act_arrival(h, i).wait_recv()
             act_copy(h, i).wait_send()
 
-    x_arrived(3)
     block = 16
     inverse = 1.0 / acts.shape[1]
 
@@ -424,12 +425,10 @@
         out_copy(j).start()
 
     for j in range(pieces):
-        own_copy(j).wait()
         core_copy(0, j).wait_recv()
         core_copy(1, j).wait_recv()
     for j in range(4):
         first(j)
-    x_arrived(4)
     x_arrived(5)
     far_arrived(0)
     for j in range(4, pieces):
@@ -466,19 +465,24 @@
             core_copy(b, j).wait_send()
 
 
-def copy_out(res_in, out_in, res_ref, out_ref, sem):
-    copies = []
-    for i, (src, dst) in enumerate(((out_in, out_ref), (res_in, res_ref))):
+def copy_out(res_in, out_in, res_ref, out_ref, res_held, out_held, load_sem, store_sem):
+    loads, stores = [], []
+    for i, (src, held, dst) in enumerate(
+        ((out_in, out_held, out_ref), (res_in, res_held, res_ref))
+    ):
         size = src.shape[0] // COPY_PARTS
         for n in range(COPY_PARTS):
             part = pl.ds(n * size, size)
-            copies.append(
-                pltpu.make_async_copy(src.at[part], dst.at[part], sem.at[i * COPY_PARTS + n])
-            )
-    for copy in copies:
-        copy.start()
-    for copy in copies:
-        copy.wait()
+            at = i * COPY_PARTS + n
+            loads.append(pltpu.make_async_copy(src.at[part], held.at[part], load_sem.at[at]))
+            stores.append(pltpu.make_async_copy(held.at[part], dst.at[part], store_sem.at[at]))
+    for load in loads:
+        load.start()
+    for load, store in zip(loads, stores):
+        load.wait()
+        store.start()
+    for store in stores:
+        store.wait()
 
 
 def on_device_kernel(
@@ -553,7 +557,12 @@
         ),
         in_specs=[anywhere] * 2,
         out_specs=(anywhere, anywhere),
-        scratch_shapes=[dma((2 * COPY_PARTS,))],
+        scratch_shapes=[
+            pltpu.VMEM((positions, chans), jnp.bfloat16),
+            pltpu.VMEM((positions, units), jnp.bfloat16),
+            dma((2 * COPY_PARTS,)),
+            dma((2 * COPY_PARTS,)),
+        ],
         compiler_params=pltpu.CompilerParams(vmem_limit_bytes=VMEM_BYTES),
     )(residual, hidden)
     return (residual.reshape(inputs.shape), hidden.reshape(1, rows, width, units))

time: 340 us -> 184 us (0.54)
  Pallas kernels: 338 us -> 182 us
    pallas_call x1, Pallas kernels: 160 us -> 4.66 us  [on_device_kernel(): pl.pallas_call(copy_out, out_shape=(jax.ShapeDtypeStruct((positions, chan...]
where the time goes in v4:
time: 184 us
  Pallas kernels  182 us (99%)
    pallas_call x1, Pallas kernels, on_device_kernel(): pl.pallas_call(functools.partial(whole_block, heads=heads, rows=rows, wid...  177 us
    pallas_call x1, Pallas kernels, on_device_kernel(): pl.pallas_call(copy_out, out_shape=(jax.ShapeDtypeStruct((positions, chan...  4.66 us

profile of v4, /device:TPU:1, one launch (start us, length us, event | category | flops | bytes accessed | tf_op | source)
XLA Modules:
  0.0 183.9 jit_solution(1225801248303026379)
XLA Ops:
  0.6 1.4 maximum_convert_fusion
  2.0 177.2 %shard_map.113 = (bf16[512,1024]{1,0:T(8,128)(2,1)}, bf16[512,4096]{1,0:T(8,128)(2,1)}) custom-call(bf16[512,1024]{1,0:T(8,128)(2,1)} %bitcast.7, bf16[512,1024]{1,0:T(8,128)(2,1)} %bitcast.8, bf16[512,1024]{1,0:T(8,128)(2,1)} %bitcast.9, bf16[512,1024]{1,0:T(8,128)(2,1)} %bitcast.10, bf16[7,7,1024]{2,1,0:T(8,128)(2,1)} %taps_ref.1, f32[1,13312]{1,0:T(1,128)} %bitcast.11, ...), custom_call_target="tpu_custom_call" | custom-call | tf_op jit(solution)/shard_map/pallas_call | solution.py:515
  179.2 4.7 %shard_map.114 = (bf16[512,1024]{1,0:T(8,128)(2,1)}, bf16[512,4096]{1,0:T(8,128)(2,1)}) custom-call(bf16[512,1024]{1,0:T(8,128)(2,1)} %get-tuple-element.6.res_in, bf16[512,4096]{1,0:T(8,128)(2,1)} %get-tuple-element.7.out_in), custom_call_target="tpu_custom_call" | custom-call | tf_op jit(solution)/shard_map/pallas_call | solution.py:552

commit v5 on v4

--- a/solution.py
+++ b/solution.py
@@ -188,6 +188,8 @@
         return [far_part(j, pl.ds(0, depth), j, True)] if j < by_y else []
 
     def far_x(j):
+        if j >= pieces:
+            return []
         if j == by_y:
             return [far_part(j, pl.ds(depth // 2, depth // 2), pieces, False)]
         return [far_part(j, pl.ds(0, depth), j, False)] if j > by_y else []
@@ -300,12 +302,14 @@
     def y_arrived(j):
         y_copy(j).wait_recv()
         core_copy(1, j).start()
-        for part in far_x(j):
-            part.start()
 
     def x_arrived(j):
         x_copy(j).wait_recv()
         for part in far_y(j):
+            part.start()
+        if 5 <= j + 3 < pieces:
+            x_copy(j + 3).start()
+        for part in far_x(j + 1):
             part.start()
         core_copy(2, j).start()
 
@@ -335,7 +339,7 @@
 
         @pl.when(h == heads)
         def _():
-            for j in range(3, pieces):
+            for j in range(3, 5):
                 x_copy(j).start()
 
         @pl.when(h >= lag)
@@ -384,41 +388,42 @@
         places.append([seq * 4 + r, seq * 4 + y, (1 - seq) * 4 + r, (1 - seq) * 4 + y])
     places = places[0] + places[1]
 
+    tile = min(256, piece)
+
     def product(here, j, slots):
         result = None
         for slot in slots:
             cols = pl.ds(pl.multiple_of(places[slot] * depth, depth), depth)
             term = jnp.dot(
-                acts[here, cols], weights[slot, j], preferred_element_type=jnp.float32
+                acts[:, cols], weights[slot, j, :, here], preferred_element_type=jnp.float32
             )
             result = term if result is None else result + term
         return result
 
-    tile = 256
-
     def first(j):
-        @pl.loop(0, positions // tile)
+        @pl.loop(0, piece // tile)
         def _(i):
             here = pl.ds(pl.multiple_of(i * tile, tile), tile)
-            total[j, here, :] = product(here, j, (0, 4, 1, 5))
+            total[j, :, here] = product(here, j, (0, 4, 1, 5))
 
     def second(j):
         core_copy(2, j).wait_recv()
 
-        @pl.loop(0, positions // tile)
+        @pl.loop(0, piece // tile)
         def _(i):
             here = pl.ds(pl.multiple_of(i * tile, tile), tile)
-            total[j, here, :] += product(here, j, (2, 6))
+            total[j, :, here] += product(here, j, (2, 6))
 
     def third(j):
         core_copy(3, j).wait_recv()
-        cols = slice(j * piece, (j + 1) * piece)
-
-        @pl.loop(0, positions // tile)
+
+        @pl.loop(0, piece // tile)
         def _(i):
             here = pl.ds(pl.multiple_of(i * tile, tile), tile)
-            value = total[j, here, :] + product(here, j, (3, 7)) + vector(ebias_at + j * piece, piece)
-            out_ref[here, cols] = (
+            cols = pl.ds(pl.multiple_of(j * piece + i * tile, tile), tile)
+            bias = pl.ds(pl.multiple_of(ebias_at + j * piece + i * tile, tile), tile)
+            value = total[j, :, here] + product(here, j, (3, 7)) + vectors_ref[:, bias]
+            out_ref[:, cols] = (
                 0.5 * value * (1.0 + lax.erf(value * (1.0 / math.sqrt(2.0))))
             ).astype(jnp.bfloat16)
 
@@ -427,13 +432,13 @@
     for j in range(pieces):
         core_copy(0, j).wait_recv()
         core_copy(1, j).wait_recv()
+    x_arrived(5)
     for j in range(4):
         first(j)
-    x_arrived(5)
     far_arrived(0)
+    x_arrived(6)
     for j in range(4, pieces):
         first(j)
-    x_arrived(6)
     far_arrived(1)
     for j in range(4):
         second(j)

time: 184 us -> 184 us (level)
  no operation moved by 1% of the time
where the time goes in v5:
time: 184 us
  Pallas kernels  182 us (99%)
    pallas_call x1, Pallas kernels, on_device_kernel(): pl.pallas_call(functools.partial(whole_block, heads=heads, rows=rows, wid...  177 us
    pallas_call x1, Pallas kernels, on_device_kernel(): pl.pallas_call(copy_out, out_shape=(jax.ShapeDtypeStruct((positions, chan...  4.66 us

profile of v5, /device:TPU:1, one launch (start us, length us, event | category | flops | bytes accessed | tf_op | source)
XLA Modules:
  0.0 183.8 jit_solution(14600011336247381601)
XLA Ops:
  0.6 1.4 maximum_convert_fusion
  2.0 177.1 %shard_map.113 = (bf16[512,1024]{1,0:T(8,128)(2,1)}, bf16[512,4096]{1,0:T(8,128)(2,1)}) custom-call(bf16[512,1024]{1,0:T(8,128)(2,1)} %bitcast.7, bf16[512,1024]{1,0:T(8,128)(2,1)} %bitcast.8, bf16[512,1024]{1,0:T(8,128)(2,1)} %bitcast.9, bf16[512,1024]{1,0:T(8,128)(2,1)} %bitcast.10, bf16[7,7,1024]{2,1,0:T(8,128)(2,1)} %taps_ref.1, f32[1,13312]{1,0:T(1,128)} %bitcast.11, ...), custom_call_target="tpu_custom_call" | custom-call | tf_op jit(solution)/shard_map/pallas_call | solution.py:520
  179.1 4.7 %shard_map.114 = (bf16[512,1024]{1,0:T(8,128)(2,1)}, bf16[512,4096]{1,0:T(8,128)(2,1)}) custom-call(bf16[512,1024]{1,0:T(8,128)(2,1)} %get-tuple-element.6.res_in, bf16[512,4096]{1,0:T(8,128)(2,1)} %get-tuple-element.7.out_in), custom_call_target="tpu_custom_call" | custom-call | tf_op jit(solution)/shard_map/pallas_call | solution.py:557

commit v6 on v5

--- a/solution.py
+++ b/solution.py
@@ -307,8 +307,6 @@
         x_copy(j).wait_recv()
         for part in far_y(j):
             part.start()
-        if 5 <= j + 3 < pieces:
-            x_copy(j + 3).start()
         for part in far_x(j + 1):
             part.start()
         core_copy(2, j).start()
@@ -325,7 +323,7 @@
             key_copy(h + ahead).start()
             value_copy(h + ahead).start()
 
-        for j, when in enumerate((2, 4, 6)):
+        for j, when in enumerate((1, 2, 4, 5, 6, 7)):
             @pl.when(h == when)
             def _():
                 x_copy(j).start()
@@ -339,8 +337,13 @@
 
         @pl.when(h == heads)
         def _():
-            for j in range(3, 5):
+            for j in range(6, pieces):
                 x_copy(j).start()
+
+        for j in range(3):
+            @pl.when(h == heads - 1 + j)
+            def _():
+                x_arrived(j)
 
         @pl.when(h >= lag)
         def _():
@@ -352,12 +355,8 @@
     res_copy.start()
     for j in range(5):
         y_arrived(j)
-    x_arrived(0)
-    y_arrived(5)
-    x_arrived(1)
-    y_arrived(6)
-    x_arrived(2)
-    y_arrived(7)
+    for j in range(5, pieces):
+        y_arrived(j)
     x_arrived(3)
     x_arrived(4)
 
@@ -575,7 +574,7 @@
 
 def solution(mesh):
     body = on_device
-    if mesh.shape["seq"] == 2 and mesh.shape["row"] == 4:
+    if (mesh.shape["seq"], mesh.shape["row"], mesh.shape["col"]) == (2, 4, 4):
         body = functools.partial(on_device_kernel, mesh.shape["col"])
     return jax.shard_map(
         body,

time: 184 us -> 187 us (1.016)
  Pallas kernels: 182 us -> 184 us
    pallas_call x1, Pallas kernels: 177 us -> 180 us  [on_device_kernel(): pl.pallas_call(functools.partial(whole_block, heads=heads, rows=rows, wid...]
where the time goes in v6:
time: 187 us; the launch traced here: 186 us
  Pallas kernels  184 us (98%)
    pallas_call x1, Pallas kernels, on_device_kernel(): pl.pallas_call(functools.partial(whole_block, heads=heads, rows=rows, wid...  180 us
    pallas_call x1, Pallas kernels, on_device_kernel(): pl.pallas_call(copy_out, out_shape=(jax.ShapeDtypeStruct((positions, chan...  4.66 us

profile of v6, /device:TPU:1, one launch (start us, length us, event | category | flops | bytes accessed | tf_op | source)
XLA Modules:
  0.0 186.5 jit_solution(5333699683453152715)
XLA Ops:
  0.6 1.4 maximum_convert_fusion
  2.0 179.8 %shard_map.113 = (bf16[512,1024]{1,0:T(8,128)(2,1)}, bf16[512,4096]{1,0:T(8,128)(2,1)}) custom-call(bf16[512,1024]{1,0:T(8,128)(2,1)} %bitcast.7, bf16[512,1024]{1,0:T(8,128)(2,1)} %bitcast.8, bf16[512,1024]{1,0:T(8,128)(2,1)} %bitcast.9, bf16[512,1024]{1,0:T(8,128)(2,1)} %bitcast.10, bf16[7,7,1024]{2,1,0:T(8,128)(2,1)} %taps_ref.1, f32[1,13312]{1,0:T(1,128)} %bitcast.11, ...), custom_call_target="tpu_custom_call" | custom-call | tf_op jit(solution)/shard_map/pallas_call | solution.py:519
  181.8 4.7 %shard_map.114 = (bf16[512,1024]{1,0:T(8,128)(2,1)}, bf16[512,4096]{1,0:T(8,128)(2,1)}) custom-call(bf16[512,1024]{1,0:T(8,128)(2,1)} %get-tuple-element.6.res_in, bf16[512,4096]{1,0:T(8,128)(2,1)} %get-tuple-element.7.out_in), custom_call_target="tpu_custom_call" | custom-call | tf_op jit(solution)/shard_map/pallas_call | solution.py:556
